TPU v7x, 256 devices: a whole 4x4x8 slice. The times are simulated.
256 devices in a mesh: wide: 64 (over z, x, core), layer: 4 (over y).
Axes of the slice: x: 4, y: 4, z: 8, core: 2. Of those that a mesh axis runs over, the one named last changes fastest.
Arguments:
- members: bfloat16 [384, 8, 32768], P('wide', 'layer'), may hold values from -6 to 6
- courant: float32 [8, 32768], P('layer'), may hold values from 0.2 to 0.9
- obs_value: float32 [2, 8, 256, 128], replicated, may hold values from -8 to 8
- obs_rinv: float32 [8, 256, 128], replicated, may hold values from 0.5 to 8
- obs_cell: int32 [8, 256, 128], replicated, may hold values from 0 to 127
- obs_count: int32 [8, 256], replicated, may hold values from 1 to 128, as said below
Outputs:
- analysis: bfloat16 [384, 8, 32768], P('wide', 'layer')
Inputs may be any that keep to these rules, and one draw needn't show every extreme that they name: `obs_count`: slots 0 to count - 1 of a level and region are live; in every draw some level and region has all 128 slots live.
All inputs are finite; a program needn't handle non-finite values.
Results may differ from a plain program's by a relative error of at most 0.0079.
The roundings to bfloat16 on the way count: a program that leaves them out, or rounds other values in their place, can miss the bound.
Values may be sent and summed in bfloat16 or wider, within the bound.
A program may use at most 64 MiB of HBM per device.

v0:
```python
import functools

import jax
import jax.numpy as jnp
from jax import lax
from jax.experimental import pallas as pl
from jax.experimental.pallas import tpu as pltpu
from jax.sharding import PartitionSpec as P

K = 384
LEV = 8
RC = 128
ITERS = 5
CYCLES = 2
F32, BF16 = jnp.float32, jnp.bfloat16
MESH = pl.DeviceIdType.MESH
PAIRS = ((0, 0), (0, 1), (0, 2), (1, 1), (1, 2), (2, 2))


def region_of(w, y):
    return 4 * w + y


def device_of(r):
    return r // 4, r % 4


def dot(a, b):
    return jnp.dot(a, b, preferred_element_type=F32)


def halves(a):
    high = a.astype(BF16)
    return high, (a - high.astype(F32)).astype(BF16)


def dot3(a, b):
    (ah, al), (bh, bl) = a, b
    return dot(ah, bh) + dot(ah, bl) + dot(al, bh)


def iota(shape, dim):
    return lax.broadcasted_iota(jnp.int32, shape, dim)


def cycles_kernel(
    st_ref, cour_ref, val_ref, rinv_ref, cell_ref, count_ref, o_ref,
    fc, sc, acc, gram, tz, xbar, hs, hr, gs, gr, vs, vr, hsem, gsem, vsem,
):
    me = region_of(lax.axis_index("wide"), lax.axis_index("layer"))
    left, right = device_of((me + 255) % 256), device_of((me + 1) % 256)
    barrier = pltpu.get_barrier_semaphore()
    for side in (left, right):
        pl.semaphore_signal(barrier, inc=1, device_id=side, device_id_type=MESH)
    pl.semaphore_wait(barrier, 2)
    o_ref[...] = st_ref[...]
    lane = iota((K, RC), 1)
    last = lane == RC - 1

    def shifted(u, before):
        return pltpu.roll(jnp.where(last, before, u), 1, axis=1)

    def cycle(c, carry):
        def edge(l, total):
            src, dst = iota((RC, RC), 0), iota((RC, RC), 1)
            pick = (src - (RC - 2) == dst - 2 * l) & (src >= RC - 2)
            return total + dot(o_ref[l], pick.astype(F32).astype(BF16))

        hs[c] = lax.fori_loop(0, LEV, edge, jnp.zeros((K, RC), F32)).astype(BF16)
        halo = pltpu.make_async_remote_copy(
            hs.at[c], hr.at[c], hsem.at[0, c], hsem.at[1, c], device_id=right, device_id_type=MESH
        )
        halo.start()
        halo.wait()
        acc[...] = jnp.zeros_like(acc)

        def level(l, carry):
            col = pl.ds(pl.multiple_of(l * RC, RC), RC)
            own = cour_ref[l, :, RC:]
            prior = cour_ref[l, :, :RC]
            before = pltpu.roll(hr[c].astype(F32), RC - 2 - 2 * l, axis=1)
            u = o_ref[l].astype(F32)
            u1 = u - own * (u - shifted(u, before))
            before1 = before - prior * (before - pltpu.roll(before, 1, axis=1))
            f = (u1 - own * (u1 - shifted(u1, before1))).astype(BF16)
            fc[l] = f
            cells = cell_ref[l]
            pick = (iota((RC, RC), 0) == cells).astype(F32).astype(BF16)
            ens = dot(f, pick)
            ybar = jnp.sum(ens, axis=0, keepdims=True) * (1.0 / K)
            anom = ens - ybar
            innov = val_ref[c, l] - ybar
            live = (iota((1, RC), 1) < count_ref[l]).astype(F32)
            for i in range(3):
                ratio = ((i - 1) * RC + cells).astype(F32) * (1.0 / RC) - (0.5 * (RC - 1)) / RC
                weight = rinv_ref[l] * jnp.exp(-(ratio * ratio)) * live
                sc[i, :, col] = (anom * jnp.sqrt(weight)).astype(BF16)
                acc[i] += anom * (weight * innov)
            return carry

        lax.fori_loop(0, LEV, level, 0)

        def gram_of(i):
            return lax.dot_general(
                sc[i], sc[i], (((1,), (1,)), ((), ())), preferred_element_type=F32
            )

        def vec_of(i):
            return jnp.sum(acc[i].T, axis=0, keepdims=True)

        sent = []
        for side, i, to in ((0, 2, left), (1, 0, right)):
            gram[...] = gram_of(i)
            for b, (p, q) in enumerate(PAIRS):
                gs[c, side, b] = gram[p * 128 : p * 128 + 128, q * 128 : q * 128 + 128]
            vs[c, side] = jnp.broadcast_to(vec_of(i), (8, K))
            for k, (src, dst, sem) in enumerate(((gs, gr, gsem), (vs, vr, vsem))):
                copy = pltpu.make_async_remote_copy(
                    src.at[c, side], dst.at[c, side], sem.at[0, c, side], sem.at[1, c, side],
                    device_id=to, device_id_type=MESH,
                )
                copy.start()
                sent.append(copy)
        gram[...] = gram_of(1)
        vec = vec_of(1)

        def parts(l, carry):
            col = pl.ds(pl.multiple_of(l * RC, RC), RC)
            f = fc[l].astype(F32)
            mean = jnp.sum(f, axis=0, keepdims=True) * (1.0 / K)
            xbar[:, col] = jnp.broadcast_to(mean, (8, RC))
            sc[0, :, col], sc[1, :, col] = halves(f - mean)
            return carry

        for copy in sent:
            copy.wait()
        lax.fori_loop(0, LEV, parts, 0)
        vec = vec + vr[c, 0, 0:1] + vr[c, 1, 0:1]
        for b, (p, q) in enumerate(PAIRS):
            block = gram[p * 128 : p * 128 + 128, q * 128 : q * 128 + 128] + gr[c, 0, b] + gr[c, 1, b]
            gram[p * 128 : p * 128 + 128, q * 128 : q * 128 + 128] = block
            if p != q:
                gram[q * 128 : q * 128 + 128, p * 128 : p * 128 + 128] = block.T
        eye = iota((K, K), 0) == iota((K, K), 1)
        amat = gram[...] + jnp.where(eye, K - 1.0, 0.0)
        scale = jnp.sqrt(jnp.sum(jnp.sum(amat * amat, axis=0, keepdims=True), axis=1, keepdims=True))
        first = amat / scale

        def advance(t):
            high, low = halves(t)
            square = dot3((high, low), (high, low))
            return 2.25 * t + dot3(halves(square), halves(0.25 * t - jnp.where(eye, 1.5, 0.0)))

        tz[1] = jnp.where(eye, 1.5, 0.0) - 0.5 * first
        tz[0] = advance(first)

        def newton(i, carry):
            t, z = tz[0], tz[1]
            tz[1] = 1.5 * z - 0.5 * dot3(halves(t), halves(z))
            tz[0] = advance(t)
            return carry

        lax.fori_loop(0, ITERS - 2, newton, 0)
        z = 1.5 * tz[1] - 0.5 * dot3(halves(tz[0]), halves(tz[1]))
        half = jnp.sum(z * vec, axis=1, keepdims=True)
        wbar = jnp.sum(z * half, axis=0, keepdims=True) / scale
        wh, wl = halves(jnp.sqrt((K - 1.0) / scale) * z + wbar)
        for j in range(LEV // 2):
            cols = slice(256 * j, 256 * j + 256)
            new = dot3((wh, wl), (sc[0, :, cols], sc[1, :, cols])) + xbar[0:1, cols]
            o_ref[2 * j] = new[:, :RC].astype(BF16)
            o_ref[2 * j + 1] = new[:, RC:].astype(BF16)
        return carry

    lax.fori_loop(0, CYCLES, cycle, 0)


def run_cycles(state, cour, values, rinv, cells, counts):
    vmem = pl.BlockSpec(memory_space=pltpu.VMEM)
    return pl.pallas_call(
        cycles_kernel,
        out_shape=jax.ShapeDtypeStruct((LEV, K, RC), BF16),
        in_specs=[vmem] * 6,
        out_specs=vmem,
        scratch_shapes=[
            pltpu.VMEM((LEV, K, RC), BF16),
            pltpu.VMEM((3, K, LEV * RC), BF16),
            pltpu.VMEM((3, K, RC), F32),
            pltpu.VMEM((K, K), F32),
            pltpu.VMEM((2, K, K), F32),
            pltpu.VMEM((8, LEV * RC), F32),
            pltpu.VMEM((CYCLES, K, RC), BF16),
            pltpu.VMEM((CYCLES, K, RC), BF16),
            pltpu.VMEM((CYCLES, 2, 6, 128, 128), F32),
            pltpu.VMEM((CYCLES, 2, 6, 128, 128), F32),
            pltpu.VMEM((CYCLES, 2, 8, K), F32),
            pltpu.VMEM((CYCLES, 2, 8, K), F32),
            pltpu.SemaphoreType.DMA((2, CYCLES)),
            pltpu.SemaphoreType.DMA((2, CYCLES, 2)),
            pltpu.SemaphoreType.DMA((2, CYCLES, 2)),
        ],
        compiler_params=pltpu.CompilerParams(
            collective_id=1, has_side_effects=True, vmem_limit_bytes=56 * 2**20
        ),
    )(state, cour, values, rinv, cells, counts)


def courant_here(courant):
    w = lax.axis_index("wide")
    extended = jnp.concatenate([courant[:, -RC:], courant], axis=1)
    near = lax.dynamic_slice_in_dim(extended, w * 4 * RC, 5 * RC, 1)
    blocks = jnp.stack([near[:, i * RC : i * RC + 2 * RC] for i in range(4)])
    return lax.all_to_all(blocks, "layer", 0, 0, tiled=True).reshape(LEV, 1, 2 * RC)


def per_device(members, courant, obs_value, obs_rinv, obs_cell, obs_count):
    region = region_of(lax.axis_index("wide"), lax.axis_index("layer"))

    def here(table, axis):
        return lax.dynamic_slice_in_dim(table, region, 1, axis)

    cour = courant_here(courant)
    counts = jnp.broadcast_to(here(obs_count, 1)[:, None], (LEV, 1, RC))
    blocks = members.reshape(6, 2, 256, RC).transpose(2, 0, 1, 3)
    blocks = lax.all_to_all(blocks, ("wide", "layer"), 0, 0, tiled=True)
    state = blocks.reshape(64, 4, 6, 2, RC).transpose(1, 3, 0, 2, 4).reshape(LEV, K, RC)
    state = run_cycles(
        state, cour, here(obs_value, 2), here(obs_rinv, 1), here(obs_cell, 1), counts
    )
    blocks = state.reshape(4, 2, 64, 6, RC).transpose(2, 0, 3, 1, 4).reshape(256, 6, 2, RC)
    blocks = lax.all_to_all(blocks, ("wide", "layer"), 0, 0, tiled=True)
    return blocks.transpose(1, 2, 0, 3).reshape(6, 2, 256 * RC)


def solution(mesh):
    placed = (P("wide", "layer", None), P("layer", None), P(), P(), P(), P())
    return jax.shard_map(
        per_device, mesh=mesh, in_specs=placed, out_specs=P("wide", "layer", None), check_vma=False
    )
```

profile of v0, /device:TPU:1, one launch (start us, length us, event | category | flops | bytes accessed | tf_op | source)
XLA Modules:
  0.0 162.2 jit_solution(7095625668731905557)
XLA Ops:
  0.0 0.8 slice.15
  0.8 0.7 fusion
  1.5 0.6 pad_maximum_fusion
  2.1 5.0 %all-to-all-start.1 = ((f32[4,2,256]{2,1,0:T(2,128)}), f32[4,2,256]{2,1,0:T(2,128)S(1)}, u32[]{:S(2)}, u32[]{:S(2)}) async-start(f32[4,2,256]{2,1,0:T(2,128)} %pad_maximum_fusion), calls=%async_computation.1 | async-start | bytes 16384 | tf_op jit(solution)/shard_map/all_to_all | solution.py:213
  7.2 2.5 %reshape.24 = bf16[6,2,256,128]{3,2,1,0:T(8,128)(2,1)S(1)} reshape(bf16[6,2,32768]{2,1,0:T(2,128)(2,1)} %param.6) | data formatting | bytes 1572864 | tf_op jit(solution)/shard_map/reshape | solution.py:224
  9.7 1.7 %copy.17 = bf16[256,6,2,128]{3,2,1,0:T(2,128)(2,1)} copy(bf16[256,6,2,128]{3,0,2,1:T(8,128)(2,1)S(1)} %bitcast.27) | data formatting | bytes 1572864 | tf_op jit(solution)/shard_map/transpose | solution.py:224
  11.4 0.0 all-to-all-done.1
  11.4 15.5 %all-to-all-start = ((bf16[256,6,2,128]{3,2,1,0:T(2,128)(2,1)}), bf16[256,6,2,128]{3,2,1,0:T(2,128)(2,1)S(1)}, u32[]{:S(2)}, u32[]{:S(2)}) async-start(bf16[256,6,2,128]{3,2,1,0:T(2,128)(2,1)} %copy.17), calls=%async_computation | async-start | bytes 1572864 | tf_op jit(solution)/shard_map/all_to_all | solution.py:225
  26.9 0.2 dynamic-slice_reduce_fusion
  27.1 1.4 constant_dynamic-slice_fusion.1.rinv_ref
  28.4 1.3 constant_dynamic-slice_fusion.cell_ref
  29.8 0.6 constant_dynamic-slice_fusion.2.val_ref
  30.4 0.6 reshape.27.cour_ref
  31.0 21.3 %all-to-all-done = bf16[256,6,2,128]{3,2,1,0:T(2,128)(2,1)S(1)} async-done(((bf16[256,6,2,128]{3,2,1,0:T(2,128)(2,1)}), bf16[256,6,2,128]{3,2,1,0:T(2,128)(2,1)S(1)}, u32[]{:S(2)}, u32[]{:S(2)}) %all-to-all-start) | async-done | bytes 786464 | tf_op jit(solution)/shard_map/all_to_all | solution.py:225
  52.3 0.1 copy.18
  52.5 1.2 copy.19
  53.7 1.0 copy.20.st_ref
  54.7 0.7 broadcast_in_dim.9.count_ref
  55.3 69.3 %shard_map.64 = bf16[8,384,128]{2,1,0:T(8,128)(2,1)} custom-call(bf16[8,384,128]{2,1,0:T(8,128)(2,1)} %copy.20.st_ref, f32[8,1,256]{2,1,0:T(1,128)} %reshape.27.cour_ref, f32[2,8,1,128]{3,2,1,0:T(1,128)} %constant_dynamic-slice_fusion.2.val_ref, f32[8,1,128]{2,1,0:T(1,128)} %constant_dynamic-slice_fusion.1.rinv_ref, ...), custom_call_target="tpu_custom_call" | custom-call | tf_op jit(solution)/shard_map/pallas_call | solution.py:180
  124.6 1.6 %copy.21 = bf16[8,384,128]{2,0,1:T(8,128)(2,1)S(1)} copy(bf16[8,384,128]{2,1,0:T(8,128)(2,1)} %shard_map.64) | data formatting | bytes 1572864 | tf_op jit(solution)/shard_map/pallas_call | solution.py:180
  126.3 0.2 copy.22
  126.5 0.8 copy.23
  127.3 33.4 %all_to_all.15 = bf16[256,6,2,128]{3,2,1,0:T(2,128)(2,1)S(1)} all-to-all(bf16[256,6,2,128]{3,2,1,0:T(2,128)(2,1)S(1)} %copy.23), channel_id=1, replica_groups=mesh['wide'=64,'layer'=4] {'wide','layer'}, dimensions={0} | all-to-all | bytes 1572864 | tf_op jit(solution)/shard_map/all_to_all | solution.py:231
  160.8 1.4 copy_bitcast_fusion
  (5 shorter events, 0.0 us)
Async XLA Ops:
  0.0 29.8 %copy-start = (f32[2,8,256,128]{3,2,1,0:T(8,128)S(1)}, f32[2,8,256,128]{3,2,1,0:T(8,128)}, u32[]{:S(2)}) copy-start(f32[2,8,256,128]{3,2,1,0:T(8,128)} %param.8) | copy-start | bytes 6291460
  2.1 9.3 %all-to-all-start.1 = ((f32[4,2,256]{2,1,0:T(2,128)}), f32[4,2,256]{2,1,0:T(2,128)S(1)}, u32[]{:S(2)}, u32[]{:S(2)}) async-start(f32[4,2,256]{2,1,0:T(2,128)} %pad_maximum_fusion), calls=%async_computation.1 | async-start | bytes 16384 | tf_op jit(solution)/shard_map/all_to_all | solution.py:213
  7.2 19.7 %copy-start.1 = (s32[8,256]{1,0:T(8,128)S(1)}, s32[8,256]{1,0:T(8,128)}, u32[]{:S(2)}) copy-start(s32[8,256]{1,0:T(8,128)} %param.11) | copy-start | bytes 24580
  11.4 40.9 %all-to-all-start = ((bf16[256,6,2,128]{3,2,1,0:T(2,128)(2,1)}), bf16[256,6,2,128]{3,2,1,0:T(2,128)(2,1)S(1)}, u32[]{:S(2)}, u32[]{:S(2)}) async-start(bf16[256,6,2,128]{3,2,1,0:T(2,128)(2,1)} %copy.17), calls=%async_computation | async-start | bytes 1572864 | tf_op jit(solution)/shard_map/all_to_all | solution.py:225
where the time goes:
time: 163 us; the launch traced here: 162 us
  Pallas kernels  69.3 us (43%)
  blocking collectives  33.4 us (20%)
  waiting for transfers between devices  21.3 us (13%)
  starting transfers between devices  20.5 us (13%)
  local copies, waits for them, and re-layouts  16.3 us (10%)
    pallas_call x1, Pallas kernels, run_cycles(): pl.pallas_call(cycles_kernel, out_shape=jax.ShapeDtypeStruct((LEV, K, RC)...  69.3 us
    all_to_all x1, blocking collectives, per_device(): blocks = lax.all_to_all(blocks, ('wide', 'layer'), 0, 0, tiled=True)  33.4 us
    all_to_all x1, waiting for transfers between devices, per_device(): blocks = lax.all_to_all(blocks, ('wide', 'layer'), 0, 0, tiled=True)  21.3 us
    all_to_all x1, starting transfers between devices, per_device(): blocks = lax.all_to_all(blocks, ('wide', 'layer'), 0, 0, tiled=True)  15.5 us
    all_to_all x1, starting transfers between devices, courant_here(): lax.all_to_all(blocks, 'layer', 0, 0, tiled=True).reshape(LEV, 1, 2 * RC)  5.01 us
    dynamic_slice x4, local copies, waits for them, and re-layouts, here(): return lax.dynamic_slice_in_dim(table, region, 1, axis)  3.5 us
  transfers between devices with their start and end apart: 2, of which 1 were waited for; matrix products, arithmetic and copies ran while one was open for 5% of the time, Pallas kernels for 0%

commit v1 on v0

v1 whole, which is shorter than its diff:
```python
import functools

import jax
import jax.numpy as jnp
from jax import lax
from jax.experimental import pallas as pl
from jax.experimental.pallas import tpu as pltpu
from jax.sharding import PartitionSpec as P

K = 384
LEV = 8
RC = 128
ITERS = 5
CYCLES = 2
F32, BF16 = jnp.float32, jnp.bfloat16
MESH = pl.DeviceIdType.MESH
CHUNKS = 2
PART = 6 // CHUNKS
PLANE = 32 * RC
PAIRS = ((0, 0), (0, 1), (0, 2), (1, 1), (1, 2), (2, 2))


def order_in_plane(z, q, y):
    a = (y + z) % 4
    return a * 8 + ((q // 2 + a) % 4) * 2 + q % 2


def device_of(r):
    z, a, b, core = r // 32, (r // 8) % 4, (r // 2) % 4, r % 2
    return z * 8 + ((b - a + 4) % 4) * 2 + core, (a - z + 8) % 4


def dot(a, b):
    return jnp.dot(a, b, preferred_element_type=F32)


def halves(a):
    high = a.astype(BF16)
    return high, (a - high.astype(F32)).astype(BF16)


def dot3(a, b):
    (ah, al), (bh, bl) = a, b
    return dot(ah, bh) + dot(ah, bl) + dot(al, bh)


def iota(shape, dim):
    return lax.broadcasted_iota(jnp.int32, shape, dim)


def whole_kernel(
    mem_ref, cour_ref, val_ref, rinv_ref, cell_ref, count_ref, o_ref,
    b1, land, leave, b2, st, near, tabv, tabr, tabc, tabn, vals, cells, roots, weights,
    fc, sc, acc, gram, tz, xbar, hs, hr, gs, gr, vs, vr,
    zin, pin, pout, zout, csem, tsem, lsem, hsem, gsem, vsem,
):
    w, y = lax.axis_index("wide"), lax.axis_index("layer")
    z, q = w // 8, w % 8
    here = order_in_plane(z, q, y)
    me = z * 32 + here
    mine = y * 8 + q
    left, right = device_of((me + 255) % 256), device_of((me + 1) % 256)

    def z_partner(s):
        z2 = (z + s) % 8
        return z2, (z2 * 8 + q, y)

    def plane_partner(s):
        q2, y2 = (q + s) % 8, (y + s // 8) % 4
        return q2, y2, (z * 8 + q2, y2)

    def cells_of(r, n=RC):
        return pl.ds(pl.multiple_of(r * RC, RC), n)

    def remote(src, dst, sems, to):
        return pltpu.make_async_remote_copy(
            src, dst, sems.at[0], sems.at[1], device_id=to, device_id_type=MESH
        )

    def drain(ref, sem):
        pltpu.make_async_copy(ref, ref, sem).wait()

    def local(src, dst, k):
        return pltpu.make_async_copy(src, dst, lsem.at[k])

    barrier = pltpu.get_barrier_semaphore()

    def greet(device):
        pl.semaphore_signal(barrier, inc=1, device_id=device, device_id_type=MESH)

    def greet_plane(s, carry):
        greet(plane_partner(s)[2])
        return carry

    def greet_z(s, carry):
        greet(z_partner(s)[1])
        return carry

    lax.fori_loop(1, 8, greet_z, 0)
    lax.fori_loop(1, 32, greet_plane, 0)
    greet(left)
    greet(right)
    row8 = pl.ds(pl.multiple_of(me // 8 * 8, 8), 8)
    tables = [
        pltpu.make_async_copy(val_ref.at[:, :, row8], tabv, tsem.at[0]),
        pltpu.make_async_copy(rinv_ref.at[:, row8], tabr, tsem.at[1]),
        pltpu.make_async_copy(cell_ref.at[:, row8], tabc, tsem.at[2]),
        pltpu.make_async_copy(count_ref, tabn, tsem.at[3]),
    ]
    for copy in tables:
        copy.start()
    own_plane = cells_of(z * 32, PLANE)
    keep = local(mem_ref.at[:, :, own_plane], b1.at[z], 0)
    keep.start()
    pl.semaphore_wait(barrier, 40)

    for ch in range(CHUNKS):
        some = pl.ds(ch * PART, PART)

        def send_z(s, carry, some=some, ch=ch):
            z2, to = z_partner(s)
            src = mem_ref.at[some, :, cells_of(z2 * 32, PLANE)]
            remote(src, b1.at[z, some], zin.at[ch], to).start()
            return carry

        lax.fori_loop(1, 8, send_z, 0)

    before_me = (me + 255) % 256
    keeps = [local(cour_ref.at[:, :, cells_of(me)], near.at[0, pl.ds(2 * y, 2)], 1),
             local(cour_ref.at[:, :, cells_of(before_me)], near.at[1, pl.ds(2 * y, 2)], 2)]
    for copy in keeps:
        copy.start()

    def send_courant(s, carry):
        y2 = (y + s) % 4
        r = z * 32 + order_in_plane(z, q, y2)
        for k, r2 in enumerate((r, (r + 255) % 256)):
            dst = near.at[k, pl.ds(2 * y, 2)]
            remote(cour_ref.at[:, :, cells_of(r2)], dst, csem.at[k], (w, y2)).start()
        return carry

    lax.fori_loop(1, 4, send_courant, 0)

    for copy in tables:
        copy.wait()
    mine8 = me % 8
    at8 = iota((8, RC), 0) == mine8
    count = jnp.sum(jnp.where(iota((LEV, 256), 1) == me, tabn[...], 0), axis=1, keepdims=True)
    live = (iota((LEV, RC), 1) < count).astype(F32)
    for l in range(LEV):
        for c in range(CYCLES):
            vals[c, l] = jnp.sum(jnp.where(at8, tabv[c, l], 0.0), axis=0, keepdims=True)
        cell = jnp.sum(jnp.where(at8, tabc[l], 0), axis=0, keepdims=True)
        cells[l] = cell
        rinv = jnp.sum(jnp.where(at8, tabr[l], 0.0), axis=0, keepdims=True)
        for i in range(3):
            ratio = (((i - 1) * RC + cell).astype(F32) - 0.5 * (RC - 1)) * (1.0 / RC)
            weight = rinv * jnp.exp(-(ratio * ratio)) * live[l : l + 1]
            weights[i, l] = weight
            roots[i, l] = jnp.sqrt(weight)
    keep.wait()

    for ch in range(CHUNKS):
        some = pl.ds(ch * PART, PART)
        drain(b1.at[pl.ds(0, 7), some], zin.at[ch, 1])

        def send_plane(s, carry, some=some, ch=ch):
            q2, y2, to = plane_partner(s)
            src = b1.at[:, some, :, cells_of(order_in_plane(z, q2, y2))]
            remote(src, land.at[mine, :, some], pin.at[ch], to).start()
            return carry

        lax.fori_loop(1, 32, send_plane, 0)
    keep = local(b1.at[:, :, :, cells_of(here)], land.at[mine], 0)
    keep.start()
    for copy in keeps:
        copy.wait()
    for k in range(2):
        drain(near.at[k, pl.ds(0, 6)], csem.at[k, 1])
    keep.wait()
    for ch in range(CHUNKS):
        drain(land.at[pl.ds(0, 31), :, pl.ds(ch * PART, PART)], pin.at[ch, 1])

    out, col = iota((256, 256), 0), iota((256, 256), 1)
    apart = (col == (out % 128) * 2 + out // 128).astype(F32).astype(BF16)
    together = (out == (col % 128) * 2 + col // 128).astype(F32).astype(BF16)

    def unpack(v, carry):
        rows = land[pl.ds(v * 8, 8)].reshape(2 * K, RC)
        for b in range(3):
            both = dot(apart, rows[256 * b : 256 * b + 256]).astype(BF16)
            st[2 * v, 128 * b : 128 * b + 128] = both[:128]
            st[2 * v + 1, 128 * b : 128 * b + 128] = both[128:]
        return carry

    lax.fori_loop(0, 4, unpack, 0)
    lane = iota((K, RC), 1)
    last = lane == RC - 1

    def shifted(u, before):
        return pltpu.roll(jnp.where(last, before, u), 1, axis=1)

    def cycle(c, carry):
        def edge(l, total):
            src, dst = iota((RC, RC), 0), iota((RC, RC), 1)
            pick = (src - (RC - 2) == dst - 2 * l) & (src >= RC - 2)
            return total + dot(st[l], pick.astype(F32).astype(BF16))

        hs[c] = lax.fori_loop(0, LEV, edge, jnp.zeros((K, RC), F32)).astype(BF16)
        halo = pltpu.make_async_remote_copy(
            hs.at[c], hr.at[c], hsem.at[0, c], hsem.at[1, c], device_id=right, device_id_type=MESH
        )
        halo.start()
        halo.wait()
        acc[...] = jnp.zeros_like(acc)

        def level(l, carry):
            col = pl.ds(pl.multiple_of(l * RC, RC), RC)
            own = near[0, l]
            prior = near[1, l]
            before = pltpu.roll(hr[c].astype(F32), RC - 2 - 2 * l, axis=1)
            u = st[l].astype(F32)
            u1 = u - own * (u - shifted(u, before))
            before1 = before - prior * (before - pltpu.roll(before, 1, axis=1))
            f = (u1 - own * (u1 - shifted(u1, before1))).astype(BF16)
            fc[l] = f
            pick = (iota((RC, RC), 0) == cells[l]).astype(F32).astype(BF16)
            ens = dot(f, pick)
            ybar = jnp.sum(ens, axis=0, keepdims=True) * (1.0 / K)
            anom = ens - ybar
            innov = vals[c, l] - ybar
            for i in range(3):
                sc[i, :, col] = (anom * roots[i, l]).astype(BF16)
                acc[i] += anom * (weights[i, l] * innov)
            return carry

        lax.fori_loop(0, LEV, level, 0)

        def gram_of(i):
            return lax.dot_general(
                sc[i], sc[i], (((1,), (1,)), ((), ())), preferred_element_type=F32
            )

        def vec_of(i):
            return jnp.sum(acc[i].T, axis=0, keepdims=True)

        sent = []
        for side, i, to in ((0, 2, left), (1, 0, right)):
            gram[...] = gram_of(i)
            for b, (p, q) in enumerate(PAIRS):
                gs[c, side, b] = gram[p * 128 : p * 128 + 128, q * 128 : q * 128 + 128]
            vs[c, side] = jnp.broadcast_to(vec_of(i), (8, K))
            for k, (src, dst, sem) in enumerate(((gs, gr, gsem), (vs, vr, vsem))):
                copy = pltpu.make_async_remote_copy(
                    src.at[c, side], dst.at[c, side], sem.at[0, c, side], sem.at[1, c, side],
                    device_id=to, device_id_type=MESH,
                )
                copy.start()
                sent.append(copy)
        gram[...] = gram_of(1)
        vec = vec_of(1)

        def parts(l, carry):
            col = pl.ds(pl.multiple_of(l * RC, RC), RC)
            f = fc[l].astype(F32)
            mean = jnp.sum(f, axis=0, keepdims=True) * (1.0 / K)
            xbar[:, col] = jnp.broadcast_to(mean, (8, RC))
            sc[0, :, col], sc[1, :, col] = halves(f - mean)
            return carry

        for copy in sent:
            copy.wait()
        lax.fori_loop(0, LEV, parts, 0)
        vec = vec + vr[c, 0, 0:1] + vr[c, 1, 0:1]
        for b, (p, q) in enumerate(PAIRS):
            block = gram[p * 128 : p * 128 + 128, q * 128 : q * 128 + 128] + gr[c, 0, b] + gr[c, 1, b]
            gram[p * 128 : p * 128 + 128, q * 128 : q * 128 + 128] = block
            if p != q:
                gram[q * 128 : q * 128 + 128, p * 128 : p * 128 + 128] = block.T
        eye = iota((K, K), 0) == iota((K, K), 1)
        amat = gram[...] + jnp.where(eye, K - 1.0, 0.0)
        scale = jnp.sqrt(jnp.sum(jnp.sum(amat * amat, axis=0, keepdims=True), axis=1, keepdims=True))
        first = amat / scale

        def advance(t):
            high, low = halves(t)
            square = dot3((high, low), (high, low))
            return 2.25 * t + dot3(halves(square), halves(0.25 * t - jnp.where(eye, 1.5, 0.0)))

        tz[1] = jnp.where(eye, 1.5, 0.0) - 0.5 * first
        tz[0] = advance(first)

        def newton(i, carry):
            t, z = tz[0], tz[1]
            tz[1] = 1.5 * z - 0.5 * dot3(halves(t), halves(z))
            tz[0] = advance(t)
            return carry

        lax.fori_loop(0, ITERS - 2, newton, 0)
        z = 1.5 * tz[1] - 0.5 * dot3(halves(tz[0]), halves(tz[1]))
        half = jnp.sum(z * vec, axis=1, keepdims=True)
        wbar = jnp.sum(z * half, axis=0, keepdims=True) / scale
        wh, wl = halves(jnp.sqrt((K - 1.0) / scale) * z + wbar)
        for j in range(LEV // 2):
            cols = slice(256 * j, 256 * j + 256)
            new = dot3((wh, wl), (sc[0, :, cols], sc[1, :, cols])) + xbar[0:1, cols]
            st[2 * j] = new[:, :RC].astype(BF16)
            st[2 * j + 1] = new[:, RC:].astype(BF16)
        return carry

    lax.fori_loop(0, CYCLES, cycle, 0)

    def pack(v, carry):
        rows = []
        for b in range(3):
            both = [st[2 * v + p, 128 * b : 128 * b + 128] for p in range(2)]
            rows.append(dot(together, jnp.concatenate(both, axis=0)).astype(BF16))
        leave[pl.ds(v * 8, 8)] = jnp.concatenate(rows, axis=0).reshape(8, 8, 6, 2, RC)
        return carry

    lax.fori_loop(0, 4, pack, 0)

    keep = local(leave.at[mine], b2.at[:, :, :, cells_of(here)], 0)
    keep.start()
    for ch in range(CHUNKS):
        some = pl.ds(ch * PART, PART)

        def return_plane(s, carry, some=some, ch=ch):
            q2, y2, to = plane_partner(s)
            dst = b2.at[:, some, :, cells_of(here)]
            remote(leave.at[y2 * 8 + q2, :, some], dst, pout.at[ch], to).start()
            return carry

        lax.fori_loop(1, 32, return_plane, 0)
    keep.wait()
    for ch in range(CHUNKS):
        some = pl.ds(ch * PART, PART)
        drain(b2.at[:, some, :, pl.ds(0, 31 * RC)], pout.at[ch, 1])

        def return_z(s, carry, some=some, ch=ch):
            z2, to = z_partner(s)
            remote(b2.at[z2, some], o_ref.at[some, :, own_plane], zout.at[ch], to).start()
            return carry

        lax.fori_loop(1, 8, return_z, 0)
    keep = local(b2.at[z], o_ref.at[:, :, own_plane], 0)
    keep.start()
    for ch in range(CHUNKS):
        some = pl.ds(ch * PART, PART)
        drain(b1.at[pl.ds(0, 7), some], zin.at[ch, 0])
        drain(land.at[pl.ds(0, 31), :, some], pin.at[ch, 0])
        drain(land.at[pl.ds(0, 31), :, some], pout.at[ch, 0])
        drain(b1.at[pl.ds(0, 7), some], zout.at[ch, 0])
        drain(o_ref.at[some, :, pl.ds(0, 7 * PLANE)], zout.at[ch, 1])
    for k in range(2):
        drain(near.at[k, pl.ds(0, 6)], csem.at[k, 0])
    keep.wait()


def per_device(members, courant, obs_value, obs_rinv, obs_cell, obs_count):
    vmem = pltpu.VMEM
    dma = pltpu.SemaphoreType.DMA
    return pl.pallas_call(
        whole_kernel,
        out_shape=jax.ShapeDtypeStruct(members.shape, BF16),
        in_specs=[pl.BlockSpec(memory_space=pl.ANY)] * 6,
        out_specs=pl.BlockSpec(memory_space=pl.ANY),
        scratch_shapes=[
            vmem((8, 6, 2, PLANE), BF16),
            vmem((32, 8, 6, 2, RC), BF16),
            vmem((32, 8, 6, 2, RC), BF16),
            vmem((8, 6, 2, PLANE), BF16),
            vmem((LEV, K, RC), BF16),
            vmem((2, LEV, 1, RC), F32),
            vmem((CYCLES, LEV, 8, RC), F32),
            vmem((LEV, 8, RC), F32),
            vmem((LEV, 8, RC), jnp.int32),
            vmem((LEV, 256), jnp.int32),
            vmem((CYCLES, LEV, 1, RC), F32),
            vmem((LEV, 1, RC), jnp.int32),
            vmem((3, LEV, 1, RC), F32),
            vmem((3, LEV, 1, RC), F32),
            vmem((LEV, K, RC), BF16),
            vmem((3, K, LEV * RC), BF16),
            vmem((3, K, RC), F32),
            vmem((K, K), F32),
            vmem((2, K, K), F32),
            vmem((8, LEV * RC), F32),
            vmem((CYCLES, K, RC), BF16),
            vmem((CYCLES, K, RC), BF16),
            vmem((CYCLES, 2, 6, 128, 128), F32),
            vmem((CYCLES, 2, 6, 128, 128), F32),
            vmem((CYCLES, 2, 8, K), F32),
            vmem((CYCLES, 2, 8, K), F32),
            dma((CHUNKS, 2)),
            dma((CHUNKS, 2)),
            dma((CHUNKS, 2)),
            dma((CHUNKS, 2)),
            dma((2, 2)),
            dma((4,)),
            dma((3,)),
            dma((2, CYCLES)),
            dma((2, CYCLES, 2)),
            dma((2, CYCLES, 2)),
        ],
        compiler_params=pltpu.CompilerParams(
            collective_id=0, has_side_effects=True, vmem_limit_bytes=56 * 2**20
        ),
    )(members, courant.reshape(2, 1, -1), obs_value, obs_rinv, obs_cell, obs_count)


def solution(mesh):
    placed = (P("wide", "layer", None), P("layer", None), P(), P(), P(), P())
    return jax.shard_map(
        per_device, mesh=mesh, in_specs=placed, out_specs=P("wide", "layer", None), check_vma=False
    )
```

time: 163 us -> 131 us (0.80)
  Pallas kernels: 69.3 us -> 126 us
  blocking collectives: 33.4 us -> 0 us
  waiting for transfers between devices: 21.3 us -> 0 us
  starting transfers between devices: 20.5 us -> 0 us
  local copies, waits for them, and re-layouts: 16.3 us -> 4.38 us
    pallas_call x1, Pallas kernels: 69.3 us -> 126 us  [per_device(): pl.pallas_call(whole_kernel, out_shape=jax.ShapeDtypeStruct(members.shape...]
    all_to_all x1 -> x0, blocking collectives: 33.4 us -> none  [per_device(): blocks = lax.all_to_all(blocks, ('wide', 'layer'), 0, 0, tiled=True)]
    all_to_all x2 -> x0, waiting for transfers between devices: 21.3 us -> none  [the longest x1 21.3 us: per_device(): blocks = lax.all_to_all(blocks, ('wide', 'layer'), 0, 0, tiled=True)]
    all_to_all x2 -> x0, starting transfers between devices: 20.5 us -> none  [the longest x1 15.5 us: per_device(): blocks = lax.all_to_all(blocks, ('wide', 'layer'), 0, 0, tiled=True)]
    reshape x5 -> x1, local copies, waits for them, and re-layouts: 6.39 us -> 1.83 us  [per_device(): courant.reshape(2, 1, -1)]
    dynamic_slice x4 -> x0, local copies, waits for them, and re-layouts: 3.5 us -> none  [here(): return lax.dynamic_slice_in_dim(table, region, 1, axis)]
    transpose x3 -> x0, local copies, waits for them, and re-layouts: 3.15 us -> none  [the longest x1 1.69 us: per_device(): blocks = members.reshape(6, 2, 256, RC).transpose(2, 0, 1, 3)]
    unnamed x4 -> x1, local copies, waits for them, and re-layouts: 0.01 us -> 2.55 us
  transfers between devices with their start and end apart: 2 -> 0, of which waited for: 1 -> 0; matrix products, arithmetic and copies ran while one was open for 5% -> 0% of each run, Pallas kernels for 0% -> 0%
where the time goes in v1:
time: 131 us
  Pallas kernels  126 us (96%)
  local copies, waits for them, and re-layouts  4.38 us (3%)
    pallas_call x1, Pallas kernels, per_device(): pl.pallas_call(whole_kernel, out_shape=jax.ShapeDtypeStruct(members.shape...  126 us

profile of v1, /device:TPU:1, one launch (start us, length us, event | category | flops | bytes accessed | tf_op | source)
XLA Modules:
  0.0 130.5 jit_solution(15097528554483786906)
XLA Ops:
  0.0 1.8 %reshape.3.cour_ref = f32[2,1,32768]{2,1,0:T(1,128)} reshape(f32[2,32768]{1,0:T(2,128)} %param.7) | data formatting | bytes 524288 | tf_op jit(solution)/shard_map/reshape | solution.py:409
  1.8 126.1 %shard_map.64 = bf16[6,2,32768]{2,1,0:T(2,128)(2,1)} custom-call(bf16[6,2,32768]{2,1,0:T(2,128)(2,1)} %mem_ref.1, f32[2,1,32768]{2,1,0:T(1,128)} %reshape.3.cour_ref, f32[2,8,256,128]{3,2,1,0:T(8,128)} %val_ref.1, f32[8,256,128]{2,1,0:T(8,128)} %rinv_ref.1, s32[8,256,128]{2,1,0:T(8,128)} %cell_ref.1, s32[8,256]{1,0:T(8,128)} %count_ref.1), custom_call_target="tpu_custom_call" | custom-call | tf_op jit(solution)/shard_map/pallas_call | solution.py:363
  128.0 2.6 %copy.8 = bf16[6,2,32768]{2,1,0:T(2,128)(2,1)} copy(bf16[6,2,32768]{2,1,0:T(2,128)(2,1)} %shard_map.64) | data formatting | bytes 1572864

commit v2 on v1

--- a/solution.py
+++ b/solution.py
@@ -14,7 +14,7 @@
 CYCLES = 2
 F32, BF16 = jnp.float32, jnp.bfloat16
 MESH = pl.DeviceIdType.MESH
-CHUNKS = 2
+CHUNKS = 3
 PART = 6 // CHUNKS
 PLANE = 32 * RC
 PAIRS = ((0, 0), (0, 1), (0, 2), (1, 1), (1, 2), (2, 2))
@@ -50,7 +50,7 @@
 
 def whole_kernel(
     mem_ref, cour_ref, val_ref, rinv_ref, cell_ref, count_ref, o_ref,
-    b1, land, leave, b2, st, near, tabv, tabr, tabc, tabn, vals, cells, roots, weights,
+    b1, land, leave, b2, st, pair, near, tabv, tabr, tabc, tabn, vals, cells, roots, weights,
     fc, sc, acc, gram, tz, xbar, hs, hr, gs, gr, vs, vr,
     zin, pin, pout, zout, csem, tsem, lsem, hsem, gsem, vsem,
 ):
@@ -126,8 +126,8 @@
         lax.fori_loop(1, 8, send_z, 0)
 
     before_me = (me + 255) % 256
-    keeps = [local(cour_ref.at[:, :, cells_of(me)], near.at[0, pl.ds(2 * y, 2)], 1),
-             local(cour_ref.at[:, :, cells_of(before_me)], near.at[1, pl.ds(2 * y, 2)], 2)]
+    keeps = [local(cour_ref.at[:, cells_of(me)], pair.at[0, y], 1),
+             local(cour_ref.at[:, cells_of(before_me)], pair.at[1, y], 2)]
     for copy in keeps:
         copy.start()
 
@@ -135,8 +135,8 @@
         y2 = (y + s) % 4
         r = z * 32 + order_in_plane(z, q, y2)
         for k, r2 in enumerate((r, (r + 255) % 256)):
-            dst = near.at[k, pl.ds(2 * y, 2)]
-            remote(cour_ref.at[:, :, cells_of(r2)], dst, csem.at[k], (w, y2)).start()
+            dst = pair.at[k, y]
+            remote(cour_ref.at[:, cells_of(r2)], dst, csem.at[k], (w, y2)).start()
         return carry
 
     lax.fori_loop(1, 4, send_courant, 0)
@@ -176,7 +176,9 @@
     for copy in keeps:
         copy.wait()
     for k in range(2):
-        drain(near.at[k, pl.ds(0, 6)], csem.at[k, 1])
+        drain(pair.at[k, pl.ds(0, 3)], csem.at[k, 1])
+        for l in range(LEV):
+            near[k, l] = pair[k, l // 2, l % 2 : l % 2 + 1]
     keep.wait()
     for ch in range(CHUNKS):
         drain(land.at[pl.ds(0, 31), :, pl.ds(ch * PART, PART)], pin.at[ch, 1])
@@ -244,12 +246,16 @@
         def vec_of(i):
             return jnp.sum(acc[i].T, axis=0, keepdims=True)
 
+        eye = iota((K, K), 0) == iota((K, K), 1)
+        eye128 = iota((128, 128), 0) == iota((128, 128), 1)
         sent = []
         for side, i, to in ((0, 2, left), (1, 0, right)):
             gram[...] = gram_of(i)
             for b, (p, q) in enumerate(PAIRS):
-                gs[c, side, b] = gram[p * 128 : p * 128 + 128, q * 128 : q * 128 + 128]
-            vs[c, side] = jnp.broadcast_to(vec_of(i), (8, K))
+                block = gram[p * 128 : p * 128 + 128, q * 128 : q * 128 + 128]
+                gs[c, side, b] = (jnp.where(eye128, 0.0, block) if p == q else block).astype(BF16)
+            diag = jnp.sum(jnp.where(eye, gram[...], 0.0), axis=0, keepdims=True)
+            vs[c, side] = jnp.where(iota((8, K), 0) == 0, vec_of(i), diag)
             for k, (src, dst, sem) in enumerate(((gs, gr, gsem), (vs, vr, vsem))):
                 copy = pltpu.make_async_remote_copy(
                     src.at[c, side], dst.at[c, side], sem.at[0, c, side], sem.at[1, c, side],
@@ -271,14 +277,16 @@
         for copy in sent:
             copy.wait()
         lax.fori_loop(0, LEV, parts, 0)
-        vec = vec + vr[c, 0, 0:1] + vr[c, 1, 0:1]
+        both = vr[c, 0] + vr[c, 1]
+        vec, diag = vec + both[0:1], both[1:2]
         for b, (p, q) in enumerate(PAIRS):
-            block = gram[p * 128 : p * 128 + 128, q * 128 : q * 128 + 128] + gr[c, 0, b] + gr[c, 1, b]
+            block = gram[p * 128 : p * 128 + 128, q * 128 : q * 128 + 128] + (
+                gr[c, 0, b].astype(F32) + gr[c, 1, b].astype(F32)
+            )
             gram[p * 128 : p * 128 + 128, q * 128 : q * 128 + 128] = block
             if p != q:
                 gram[q * 128 : q * 128 + 128, p * 128 : p * 128 + 128] = block.T
-        eye = iota((K, K), 0) == iota((K, K), 1)
-        amat = gram[...] + jnp.where(eye, K - 1.0, 0.0)
+        amat = gram[...] + jnp.where(eye, diag + (K - 1.0), 0.0)
         scale = jnp.sqrt(jnp.sum(jnp.sum(amat * amat, axis=0, keepdims=True), axis=1, keepdims=True))
         first = amat / scale
 
@@ -353,7 +361,7 @@
         drain(b1.at[pl.ds(0, 7), some], zout.at[ch, 0])
         drain(o_ref.at[some, :, pl.ds(0, 7 * PLANE)], zout.at[ch, 1])
     for k in range(2):
-        drain(near.at[k, pl.ds(0, 6)], csem.at[k, 0])
+        drain(pair.at[k, pl.ds(0, 3)], csem.at[k, 0])
     keep.wait()
 
 
@@ -371,6 +379,7 @@
             vmem((32, 8, 6, 2, RC), BF16),
             vmem((8, 6, 2, PLANE), BF16),
             vmem((LEV, K, RC), BF16),
+            vmem((2, 4, 2, RC), F32),
             vmem((2, LEV, 1, RC), F32),
             vmem((CYCLES, LEV, 8, RC), F32),
             vmem((LEV, 8, RC), F32),
@@ -388,8 +397,8 @@
             vmem((8, LEV * RC), F32),
             vmem((CYCLES, K, RC), BF16),
             vmem((CYCLES, K, RC), BF16),
-            vmem((CYCLES, 2, 6, 128, 128), F32),
-            vmem((CYCLES, 2, 6, 128, 128), F32),
+            vmem((CYCLES, 2, 6, 128, 128), BF16),
+            vmem((CYCLES, 2, 6, 128, 128), BF16),
             vmem((CYCLES, 2, 8, K), F32),
             vmem((CYCLES, 2, 8, K), F32),
             dma((CHUNKS, 2)),
@@ -406,7 +415,7 @@
         compiler_params=pltpu.CompilerParams(
             collective_id=0, has_side_effects=True, vmem_limit_bytes=56 * 2**20
         ),
-    )(members, courant.reshape(2, 1, -1), obs_value, obs_rinv, obs_cell, obs_count)
+    )(members, courant, obs_value, obs_rinv, obs_cell, obs_count)
 
 
 def solution(mesh):

time: 131 us -> 120 us (0.916)
  Pallas kernels: 126 us -> 118 us
  local copies, waits for them, and re-layouts: 4.38 us -> 2.55 us
    pallas_call x1, Pallas kernels: 126 us -> 118 us  [per_device(): pl.pallas_call(whole_kernel, out_shape=jax.ShapeDtypeStruct(members.shape...]
    reshape x1 -> x0, local copies, waits for them, and re-layouts: 1.83 us -> none  [per_device(): courant.reshape(2, 1, -1)]
where the time goes in v2:
time: 120 us
  Pallas kernels  118 us (98%)
  local copies, waits for them, and re-layouts  2.55 us (2%)
    pallas_call x1, Pallas kernels, per_device(): pl.pallas_call(whole_kernel, out_shape=jax.ShapeDtypeStruct(members.shape...  118 us
    unnamed x1, local copies, waits for them, and re-layouts  2.55 us

profile of v2, /device:TPU:1, one launch (start us, length us, event | category | flops | bytes accessed | tf_op | source)
XLA Modules:
  0.0 120.3 jit_solution(5166916365344217818)
XLA Ops:
  0.0 117.7 %shard_map.64 = bf16[6,2,32768]{2,1,0:T(2,128)(2,1)} custom-call(bf16[6,2,32768]{2,1,0:T(2,128)(2,1)} %mem_ref.1, f32[2,32768]{1,0:T(2,128)} %cour_ref.1, f32[2,8,256,128]{3,2,1,0:T(8,128)} %val_ref.1, f32[8,256,128]{2,1,0:T(8,128)} %rinv_ref.1, s32[8,256,128]{2,1,0:T(8,128)} %cell_ref.1, s32[8,256]{1,0:T(8,128)} %count_ref.1), custom_call_target="tpu_custom_call" | custom-call | tf_op jit(solution)/shard_map/pallas_call | solution.py:371
  117.7 2.6 %copy.8 = bf16[6,2,32768]{2,1,0:T(2,128)(2,1)} copy(bf16[6,2,32768]{2,1,0:T(2,128)(2,1)} %shard_map.64) | data formatting | bytes 1572864

commit v3 on v2

--- a/solution.py
+++ b/solution.py
@@ -202,18 +202,21 @@
     def shifted(u, before):
         return pltpu.roll(jnp.where(last, before, u), 1, axis=1)
 
+    def pick_edge(l):
+        src, dst = iota((RC, RC), 0), iota((RC, RC), 1)
+        return ((src - (RC - 2) == dst - 2 * l) & (src >= RC - 2)).astype(F32).astype(BF16)
+
+    def halo(c):
+        return remote(hs.at[c], hr.at[c], hsem.at[c], right)
+
+    def edge(l, total):
+        return total + dot(st[l], pick_edge(l))
+
+    hs[0] = lax.fori_loop(0, LEV, edge, jnp.zeros((K, RC), F32)).astype(BF16)
+    halo(0).start()
+
     def cycle(c, carry):
-        def edge(l, total):
-            src, dst = iota((RC, RC), 0), iota((RC, RC), 1)
-            pick = (src - (RC - 2) == dst - 2 * l) & (src >= RC - 2)
-            return total + dot(st[l], pick.astype(F32).astype(BF16))
-
-        hs[c] = lax.fori_loop(0, LEV, edge, jnp.zeros((K, RC), F32)).astype(BF16)
-        halo = pltpu.make_async_remote_copy(
-            hs.at[c], hr.at[c], hsem.at[0, c], hsem.at[1, c], device_id=right, device_id_type=MESH
-        )
-        halo.start()
-        halo.wait()
+        halo(c).wait()
         acc[...] = jnp.zeros_like(acc)
 
         def level(l, carry):
@@ -267,16 +270,24 @@
         vec = vec_of(1)
 
         def parts(l, carry):
+            high_edge, low_edge, mean_edge = carry
             col = pl.ds(pl.multiple_of(l * RC, RC), RC)
             f = fc[l].astype(F32)
             mean = jnp.sum(f, axis=0, keepdims=True) * (1.0 / K)
             xbar[:, col] = jnp.broadcast_to(mean, (8, RC))
-            sc[0, :, col], sc[1, :, col] = halves(f - mean)
-            return carry
-
+            high, low = halves(f - mean)
+            sc[0, :, col], sc[1, :, col] = high, low
+            pick = pick_edge(l)
+            moved = pltpu.roll(jnp.broadcast_to(mean, (8, RC)), 2 * l + 2, axis=1)
+            mean_edge = jnp.where(iota((8, RC), 1) // 2 == l, moved, mean_edge)
+            return high_edge + dot(high, pick), low_edge + dot(low, pick), mean_edge
+
+        zero = jnp.zeros((K, RC), F32)
+        he, le, mean_edge = lax.fori_loop(
+            0, LEV, parts, (zero, zero, jnp.zeros((8, RC), F32))
+        )
         for copy in sent:
             copy.wait()
-        lax.fori_loop(0, LEV, parts, 0)
         both = vr[c, 0] + vr[c, 1]
         vec, diag = vec + both[0:1], both[1:2]
         for b, (p, q) in enumerate(PAIRS):
@@ -290,25 +301,35 @@
         scale = jnp.sqrt(jnp.sum(jnp.sum(amat * amat, axis=0, keepdims=True), axis=1, keepdims=True))
         first = amat / scale
 
-        def advance(t):
-            high, low = halves(t)
-            square = dot3((high, low), (high, low))
-            return 2.25 * t + dot3(halves(square), halves(0.25 * t - jnp.where(eye, 1.5, 0.0)))
+        def advance(t, times):
+            return 2.25 * t + times(times(t, t), 0.25 * t - jnp.where(eye, 1.5, 0.0))
+
+        def once(a, b):
+            return dot(a.astype(BF16), b.astype(BF16))
+
+        def thrice(a, b):
+            return dot3(halves(a), halves(b))
+
+        def newton(times):
+            t, z = tz[0], tz[1]
+            tz[1] = 1.5 * z - 0.5 * times(t, z)
+            tz[0] = advance(t, times)
+
+        def newton3(i, carry):
+            newton(thrice)
+            return carry
 
         tz[1] = jnp.where(eye, 1.5, 0.0) - 0.5 * first
-        tz[0] = advance(first)
-
-        def newton(i, carry):
-            t, z = tz[0], tz[1]
-            tz[1] = 1.5 * z - 0.5 * dot3(halves(t), halves(z))
-            tz[0] = advance(t)
-            return carry
-
-        lax.fori_loop(0, ITERS - 2, newton, 0)
-        z = 1.5 * tz[1] - 0.5 * dot3(halves(tz[0]), halves(tz[1]))
+        tz[0] = advance(first, once)
+        newton(once)
+        lax.fori_loop(0, ITERS - 3, newton3, 0)
+        z = 1.5 * tz[1] - 0.5 * thrice(tz[0], tz[1])
         half = jnp.sum(z * vec, axis=1, keepdims=True)
         wbar = jnp.sum(z * half, axis=0, keepdims=True) / scale
         wh, wl = halves(jnp.sqrt((K - 1.0) / scale) * z + wbar)
+        edges = dot3((wh, wl), (he.astype(BF16), le.astype(BF16))) + mean_edge[0:1]
+        hs[c + 1] = edges.astype(BF16)
+        halo(c + 1).start()
         for j in range(LEV // 2):
             cols = slice(256 * j, 256 * j + 256)
             new = dot3((wh, wl), (sc[0, :, cols], sc[1, :, cols])) + xbar[0:1, cols]
@@ -362,6 +383,7 @@
         drain(o_ref.at[some, :, pl.ds(0, 7 * PLANE)], zout.at[ch, 1])
     for k in range(2):
         drain(pair.at[k, pl.ds(0, 3)], csem.at[k, 0])
+    halo(CYCLES).wait()
     keep.wait()
 
 
@@ -395,8 +417,8 @@
             vmem((K, K), F32),
             vmem((2, K, K), F32),
             vmem((8, LEV * RC), F32),
-            vmem((CYCLES, K, RC), BF16),
-            vmem((CYCLES, K, RC), BF16),
+            vmem((CYCLES + 1, K, RC), BF16),
+            vmem((CYCLES + 1, K, RC), BF16),
             vmem((CYCLES, 2, 6, 128, 128), BF16),
             vmem((CYCLES, 2, 6, 128, 128), BF16),
             vmem((CYCLES, 2, 8, K), F32),
@@ -408,7 +430,7 @@
             dma((2, 2)),
             dma((4,)),
             dma((3,)),
-            dma((2, CYCLES)),
+            dma((CYCLES + 1, 2)),
             dma((2, CYCLES, 2)),
             dma((2, CYCLES, 2)),
         ],

time: 120 us -> 113 us (0.942)
  Pallas kernels: 118 us -> 111 us
    pallas_call x1, Pallas kernels: 118 us -> 111 us  [per_device(): pl.pallas_call(whole_kernel, out_shape=jax.ShapeDtypeStruct(members.shape...]
where the time goes in v3:
time: 113 us
  Pallas kernels  111 us (98%)
  local copies, waits for them, and re-layouts  2.55 us (2%)
    pallas_call x1, Pallas kernels, per_device(): pl.pallas_call(whole_kernel, out_shape=jax.ShapeDtypeStruct(members.shape...  111 us
    unnamed x1, local copies, waits for them, and re-layouts  2.55 us

profile of v3, /device:TPU:1, one launch (start us, length us, event | category | flops | bytes accessed | tf_op | source)
XLA Modules:
  0.0 113.2 jit_solution(16175381246711315408)
XLA Ops:
  0.0 110.6 %shard_map.64 = bf16[6,2,32768]{2,1,0:T(2,128)(2,1)} custom-call(bf16[6,2,32768]{2,1,0:T(2,128)(2,1)} %mem_ref.1, f32[2,32768]{1,0:T(2,128)} %cour_ref.1, f32[2,8,256,128]{3,2,1,0:T(8,128)} %val_ref.1, f32[8,256,128]{2,1,0:T(8,128)} %rinv_ref.1, s32[8,256,128]{2,1,0:T(8,128)} %cell_ref.1, s32[8,256]{1,0:T(8,128)} %count_ref.1), custom_call_target="tpu_custom_call" | custom-call | tf_op jit(solution)/shard_map/pallas_call | solution.py:393
  110.6 2.6 %copy.8 = bf16[6,2,32768]{2,1,0:T(2,128)(2,1)} copy(bf16[6,2,32768]{2,1,0:T(2,128)(2,1)} %shard_map.64) | data formatting | bytes 1572864

commit v4 on v3

--- a/solution.py
+++ b/solution.py
@@ -14,7 +14,8 @@
 CYCLES = 2
 F32, BF16 = jnp.float32, jnp.bfloat16
 MESH = pl.DeviceIdType.MESH
-CHUNKS = 3
+CHUNKS = 6
+Z_ORDER = (4, 3, 5, 2, 6, 1, 7)
 PART = 6 // CHUNKS
 PLANE = 32 * RC
 PAIRS = ((0, 0), (0, 1), (0, 2), (1, 1), (1, 2), (2, 2))
@@ -41,7 +42,7 @@
 
 def dot3(a, b):
     (ah, al), (bh, bl) = a, b
-    return dot(ah, bh) + dot(ah, bl) + dot(al, bh)
+    return dot(jnp.concatenate([ah, ah, al], 1), jnp.concatenate([bh, bl, bh], 0))
 
 
 def iota(shape, dim):
@@ -66,6 +67,7 @@
         return z2, (z2 * 8 + q, y)
 
     def plane_partner(s):
+        s = (s * 13) % 32
         q2, y2 = (q + s) % 8, (y + s // 8) % 4
         return q2, y2, (z * 8 + q2, y2)
 
@@ -123,7 +125,8 @@
             remote(src, b1.at[z, some], zin.at[ch], to).start()
             return carry
 
-        lax.fori_loop(1, 8, send_z, 0)
+        for s in Z_ORDER:
+            send_z(s, 0)
 
     before_me = (me + 255) % 256
     keeps = [local(cour_ref.at[:, cells_of(me)], pair.at[0, y], 1),
@@ -312,8 +315,9 @@
 
         def newton(times):
             t, z = tz[0], tz[1]
-            tz[1] = 1.5 * z - 0.5 * times(t, z)
-            tz[0] = advance(t, times)
+            both = times(t, jnp.concatenate([t, z], axis=1))
+            tz[1] = 1.5 * z - 0.5 * both[:, K:]
+            tz[0] = 2.25 * t + times(both[:, :K], 0.25 * t - jnp.where(eye, 1.5, 0.0))
 
         def newton3(i, carry):
             newton(thrice)
@@ -371,7 +375,8 @@
             remote(b2.at[z2, some], o_ref.at[some, :, own_plane], zout.at[ch], to).start()
             return carry
 
-        lax.fori_loop(1, 8, return_z, 0)
+        for s in Z_ORDER:
+            return_z(s, 0)
     keep = local(b2.at[z], o_ref.at[:, :, own_plane], 0)
     keep.start()
     for ch in range(CHUNKS):

time: 113 us -> 109 us (0.965)
  Pallas kernels: 111 us -> 106 us
    pallas_call x1, Pallas kernels: 111 us -> 106 us  [per_device(): pl.pallas_call(whole_kernel, out_shape=jax.ShapeDtypeStruct(members.shape...]
where the time goes in v4:
time: 109 us
  Pallas kernels  106 us (97%)
  local copies, waits for them, and re-layouts  2.55 us (2%)
    pallas_call x1, Pallas kernels, per_device(): pl.pallas_call(whole_kernel, out_shape=jax.ShapeDtypeStruct(members.shape...  106 us
    unnamed x1, local copies, waits for them, and re-layouts  2.55 us

profile of v4, /device:TPU:1, one launch (start us, length us, event | category | flops | bytes accessed | tf_op | source)
XLA Modules:
  0.0 108.7 jit_solution(230197993287828626)
XLA Ops:
  0.0 106.1 %shard_map.64 = bf16[6,2,32768]{2,1,0:T(2,128)(2,1)} custom-call(bf16[6,2,32768]{2,1,0:T(2,128)(2,1)} %mem_ref.1, f32[2,32768]{1,0:T(2,128)} %cour_ref.1, f32[2,8,256,128]{3,2,1,0:T(8,128)} %val_ref.1, f32[8,256,128]{2,1,0:T(8,128)} %rinv_ref.1, s32[8,256,128]{2,1,0:T(8,128)} %cell_ref.1, s32[8,256]{1,0:T(8,128)} %count_ref.1), custom_call_target="tpu_custom_call" | custom-call | tf_op jit(solution)/shard_map/pallas_call | solution.py:398
  106.1 2.6 %copy.8 = bf16[6,2,32768]{2,1,0:T(2,128)(2,1)} copy(bf16[6,2,32768]{2,1,0:T(2,128)(2,1)} %shard_map.64) | data formatting | bytes 1572864

commit v5 on v4

--- a/solution.py
+++ b/solution.py
@@ -326,7 +326,8 @@
         tz[1] = jnp.where(eye, 1.5, 0.0) - 0.5 * first
         tz[0] = advance(first, once)
         newton(once)
-        lax.fori_loop(0, ITERS - 3, newton3, 0)
+        newton(once)
+        lax.fori_loop(0, ITERS - 4, newton3, 0)
         z = 1.5 * tz[1] - 0.5 * thrice(tz[0], tz[1])
         half = jnp.sum(z * vec, axis=1, keepdims=True)
         wbar = jnp.sum(z * half, axis=0, keepdims=True) / scale

time: 109 us -> 107 us (0.982)
  Pallas kernels: 106 us -> 104 us
    pallas_call x1, Pallas kernels: 106 us -> 104 us  [per_device(): pl.pallas_call(whole_kernel, out_shape=jax.ShapeDtypeStruct(members.shape...]
where the time goes in v5:
time: 107 us
  Pallas kernels  104 us (97%)
  local copies, waits for them, and re-layouts  2.55 us (2%)
    pallas_call x1, Pallas kernels, per_device(): pl.pallas_call(whole_kernel, out_shape=jax.ShapeDtypeStruct(members.shape...  104 us
    unnamed x1, local copies, waits for them, and re-layouts  2.55 us

profile of v5, /device:TPU:1, one launch (start us, length us, event | category | flops | bytes accessed | tf_op | source)
XLA Modules:
  0.0 106.6 jit_solution(12948373739477593828)
XLA Ops:
  0.0 104.0 %shard_map.64 = bf16[6,2,32768]{2,1,0:T(2,128)(2,1)} custom-call(bf16[6,2,32768]{2,1,0:T(2,128)(2,1)} %mem_ref.1, f32[2,32768]{1,0:T(2,128)} %cour_ref.1, f32[2,8,256,128]{3,2,1,0:T(8,128)} %val_ref.1, f32[8,256,128]{2,1,0:T(8,128)} %rinv_ref.1, s32[8,256,128]{2,1,0:T(8,128)} %cell_ref.1, s32[8,256]{1,0:T(8,128)} %count_ref.1), custom_call_target="tpu_custom_call" | custom-call | tf_op jit(solution)/shard_map/pallas_call | solution.py:399
  104.0 2.6 %copy.8 = bf16[6,2,32768]{2,1,0:T(2,128)(2,1)} copy(bf16[6,2,32768]{2,1,0:T(2,128)(2,1)} %shard_map.64) | data formatting | bytes 1572864

commit v6 on v5

--- a/solution.py
+++ b/solution.py
@@ -242,7 +242,7 @@
                 acc[i] += anom * (weights[i, l] * innov)
             return carry
 
-        lax.fori_loop(0, LEV, level, 0)
+        lax.fori_loop(0, LEV, level, 0, unroll=2)
 
         def gram_of(i):
             return lax.dot_general(

time: 107 us -> 104 us (0.972)
  Pallas kernels: 104 us -> 102 us
    pallas_call x1, Pallas kernels: 104 us -> 102 us  [per_device(): pl.pallas_call(whole_kernel, out_shape=jax.ShapeDtypeStruct(members.shape...]
where the time goes in v6:
time: 104 us
  Pallas kernels  102 us (98%)
  local copies, waits for them, and re-layouts  2.55 us (2%)
    pallas_call x1, Pallas kernels, per_device(): pl.pallas_call(whole_kernel, out_shape=jax.ShapeDtypeStruct(members.shape...  102 us
    unnamed x1, local copies, waits for them, and re-layouts  2.55 us

profile of v6, /device:TPU:1, one launch (start us, length us, event | category | flops | bytes accessed | tf_op | source)
XLA Modules:
  0.0 104.1 jit_solution(13880976080512094858)
XLA Ops:
  0.0 101.5 %shard_map.64 = bf16[6,2,32768]{2,1,0:T(2,128)(2,1)} custom-call(bf16[6,2,32768]{2,1,0:T(2,128)(2,1)} %mem_ref.1, f32[2,32768]{1,0:T(2,128)} %cour_ref.1, f32[2,8,256,128]{3,2,1,0:T(8,128)} %val_ref.1, f32[8,256,128]{2,1,0:T(8,128)} %rinv_ref.1, s32[8,256,128]{2,1,0:T(8,128)} %cell_ref.1, s32[8,256]{1,0:T(8,128)} %count_ref.1), custom_call_target="tpu_custom_call" | custom-call | tf_op jit(solution)/shard_map/pallas_call | solution.py:399
  101.5 2.6 %copy.8 = bf16[6,2,32768]{2,1,0:T(2,128)(2,1)} copy(bf16[6,2,32768]{2,1,0:T(2,128)(2,1)} %shard_map.64) | data formatting | bytes 1572864
